TPU v7x, 32 devices: a whole 2x2x4 slice. The times are simulated.
32 devices in a mesh: group: 8 (over z, x), member: 4 (over y, core).
Axes of the slice: x: 2, y: 2, z: 4, core: 2. Of those that a mesh axis runs over, the one named last changes fastest.
Arguments:
- prompt_k: bfloat16 [8, 256, 1024], P('group', 'member'), may hold values from -6 to 6
- prompt_v: bfloat16 [8, 256, 1024], P('group', 'member'), may hold values from -18 to 18
- resp_q: bfloat16 [8, 4, 128, 4096], P('group', 'member'), may hold values from -45 to 45
- resp_k: bfloat16 [8, 4, 128, 1024], P('group', 'member'), may hold values from -6 to 6
- resp_v: bfloat16 [8, 4, 128, 1024], P('group', 'member'), may hold values from -18 to 18
- out_grad: bfloat16 [8, 4, 128, 4096], P('group', 'member'), may hold values from -6 to 6
- lengths: int32 [8, 4], P('group', 'member'), may hold values from 16 to 128, as said below
- rewards: float32 [8, 4], P('group', 'member'), may hold values from -6 to 6
Outputs:
- attended: bfloat16 [8, 4, 128, 4096], P('group', 'member')
- grad_q: bfloat16 [8, 4, 128, 4096], P('group', 'member')
- grad_resp_k: bfloat16 [8, 4, 128, 1024], P('group', 'member')
- grad_resp_v: bfloat16 [8, 4, 128, 1024], P('group', 'member')
- grad_prompt_k: bfloat16 [8, 256, 1024], P('group', 'member')
- grad_prompt_v: bfloat16 [8, 256, 1024], P('group', 'member')
Inputs may be any that keep to these rules, and one draw needn't show every extreme that they name: In each group the lengths never fall from one member to the next, and the last member's response has exactly 128 live tokens.
All inputs are finite; a program needn't handle non-finite values.
Results may differ from a plain program's by a relative error of at most 0.0082.
Values may be sent and summed in bfloat16 or wider, within the bound.
A program may use at most 128 MiB of HBM per device.

v0:
```python
import functools

import jax
import jax.numpy as jnp
from jax import lax
from jax.experimental import pallas as pl
from jax.experimental.pallas import tpu as pltpu
from jax.sharding import PartitionSpec as P

KVH = 8
HD = 128
LOG2E = 1.4426950408889634
MESH = pl.DeviceIdType.MESH
NT = (((1,), (1,)), ((), ()))
NN = (((1,), (0,)), ((), ()))
TN = (((0,), (0,)), ((), ()))


def dot(a, b, dims):
    return lax.dot_general(a, b, dims, preferred_element_type=jnp.float32)


def kernel(
    groups, members, rows, slots, per_head,
    length_ref, reward_ref, pk_ref, pv_ref, q_ref, rk_ref, rv_ref, og_ref,
    att_out, gq_out, grk_out, grv_out, gpk_out, gpv_out,
    kall, vall, qbuf, obuf, att, gq, grk, grv, grk_low, grv_low, gpk, gpv,
    probs0, probs1, dsc0, dsc1,
    part, sib_send, sib_recv, x_send, x_recv, stat_send, stat, tok_send, tok,
    in_sem, g_send, f_send, g_recv, s_send, s_recv, t_send, t_recv,
    r_send, r_recv, c_send, c_recv, out_sem, end_sem,
):
    chips = members // 2
    prompt = members * rows
    wide = per_head * slots
    score_scale = float(HD) ** (-0.5)
    group = lax.axis_index("group")
    me = lax.axis_index("member")
    chip = lax.div(me, 2)
    core = lax.rem(me, 2)
    sib = chip * 2 + (1 - core)

    def chip_at(d):
        return lax.rem(chip + d, chips)

    def cols(j, width=HD):
        return pl.ds(pl.multiple_of(j * width, width), width)

    def block_rows(owner):
        return pl.ds(pl.multiple_of(owner * rows, rows), rows)

    def local(src, dst, sem):
        return pltpu.make_async_copy(src, dst, sem)

    def remote(src, dst, send, recv, to_group, to_member):
        return pltpu.make_async_remote_copy(
            src_ref=src, dst_ref=dst, send_sem=send, recv_sem=recv,
            device_id=(to_group, to_member), device_id_type=MESH)

    loads = [
        local(pk_ref.at[0], kall.at[block_rows(me)], in_sem.at[0]),
        local(pv_ref.at[0], vall.at[block_rows(me)], in_sem.at[1]),
        local(rk_ref.at[0, 0], kall.at[pl.ds(prompt, slots)], in_sem.at[2]),
        local(rv_ref.at[0, 0], vall.at[pl.ds(prompt, slots)], in_sem.at[3]),
        local(q_ref.at[0, 0], qbuf, in_sem.at[4]),
        local(og_ref.at[0, 0], obuf, in_sem.at[5]),
    ]
    for load in loads:
        load.start()

    barrier = pltpu.get_barrier_semaphore()
    for step in range(1, members):
        pl.semaphore_signal(barrier, inc=1, device_id=(group, lax.rem(me + step, members)), device_id_type=MESH)
    nodes = groups // 2
    node = lax.div(group, 2)
    twin = node * 2 + (1 - lax.rem(group, 2))
    pl.semaphore_signal(barrier, inc=1, device_id=(twin, me), device_id_type=MESH)

    @pl.when(node > 0)
    def _():
        pl.semaphore_signal(barrier, inc=1, device_id=(group - 2, me), device_id_type=MESH)

    @pl.when(node < nodes - 1)
    def _():
        pl.semaphore_signal(barrier, inc=1, device_id=(group + 2, me), device_id_type=MESH)


    length = length_ref[0, 0]
    stat_send[0] = jnp.full((8, HD), length.astype(jnp.float32))
    stat_send[1] = jnp.full((8, HD), reward_ref[0, 0])
    stat[me] = stat_send[...]
    ends = (node == 0).astype(jnp.int32) + (node == nodes - 1).astype(jnp.int32)
    pl.semaphore_wait(barrier, members + 2 - ends)

    sides = ((pk_ref, kall), (pv_ref, vall))

    def direct(side, j, slot):
        to = sib if slot == 0 else chip_at(slot) * 2 + core
        source, whole = sides[side]
        return remote(source.at[0, :, cols(j)], whole.at[block_rows(me), cols(j)],
                      g_send.at[side, j, slot], g_recv.at[side, j, me], group, to)

    def arrival(side, j, owner):
        place = sides[side][1].at[block_rows(owner), cols(j)]
        return remote(place, place, g_send.at[side, j, 0], g_recv.at[side, j, owner], group, sib)

    def forward(side, j, d):
        owner = chip_at(d) * 2 + core
        place = sides[side][1].at[block_rows(owner), cols(j)]
        return remote(place, place, f_send.at[side, j, d - 1], g_recv.at[side, j, owner], group, sib)

    def stat_copy(step):
        return remote(stat_send, stat.at[me], s_send.at[step - 1], s_recv.at[me], group, lax.rem(me + step, members))

    def tok_copy(kind):
        to = (twin, group + 2, group - 2)[kind]
        return remote(tok_send.at[kind], tok.at[kind], t_send.at[kind], t_recv.at[kind], to, me)

    def relay(slot):
        @pl.when(node == slot)
        def _():
            @pl.when(node > 0)
            def _():
                tok_copy(1).wait_recv()
                tok_send[1] = tok[1] + tok[3]

            @pl.when(node == 0)
            def _():
                tok_send[1] = tok[3]

            @pl.when(node < nodes - 1)
            def _():
                tok_copy(1).start()

        @pl.when(node == nodes - 1 - slot)
        def _():
            @pl.when(node < nodes - 1)
            def _():
                tok_copy(2).wait_recv()
                tok_send[2] = tok[2] + tok[3]

            @pl.when(node == nodes - 1)
            def _():
                tok_send[2] = tok[3]

            @pl.when(node > 0)
            def _():
                tok_copy(2).start()

    def far(side, d):
        source, whole = sides[side]
        return remote(source.at[0, :, cols(0)], whole.at[block_rows(me), cols(0)],
                      f_send.at[side, 0, d - 1], g_recv.at[side, 0, me], group, chip_at(d) * 2 + (1 - core))

    def send_head(j, carry):
        for slot in list(range(1, chips)) + [0]:
            for side in range(2):
                direct(side, j, slot).start()
        return carry

    send_head(0, 0)
    for d in range(1, chips):
        for side in range(2):
            far(side, d).start()
    for step in range(1, members):
        stat_copy(step).start()
    lax.fori_loop(1, KVH, send_head, 0)

    def forward_head(j):
        for d in range(1, chips):
            owner = chip_at(d) * 2 + core
            for side in range(2):
                arrival(side, j, owner).wait_recv()
                forward(side, j, d).start()

    def wait_head(j):
        for side in range(2):
            arrival(side, j, sib).wait_recv()
            for d in range(1, chips):
                arrival(side, j, chip_at(d) * 2 + (1 - core)).wait_recv()

    u_pos = lax.broadcasted_iota(jnp.int32, (slots, wide), 0)
    t_pos = lax.rem(lax.broadcasted_iota(jnp.int32, (slots, wide), 1), slots)
    causal = u_pos <= t_pos
    live_lane = lax.rem(lax.broadcasted_iota(jnp.int32, (HD, wide), 1), slots) < length
    live_row = lax.broadcasted_iota(jnp.int32, (slots, per_head * HD), 0) < length

    for load in loads:
        load.wait()

    def mask_head(j, carry):
        g = obuf[:, cols(j, per_head * HD)]
        obuf[:, cols(j, per_head * HD)] = jnp.where(live_row, g, jnp.zeros_like(g))
        return carry

    lax.fori_loop(0, KVH, mask_head, 0)

    def sib_copy(j):
        return remote(sib_send.at[j], sib_recv.at[j], r_send.at[j], r_recv.at[j], group, sib)

    def cross_copy(j, d):
        return remote(x_send.at[j, d - 1], x_recv.at[j, d - 1], c_send.at[j, d - 1], c_recv.at[j, d - 1],
                      group, chip_at(d) * 2 + core)

    def cross_head(j):
        sib_copy(j).wait_recv()
        for d in range(1, chips):
            own = part[j, chip_at(d) * 2 + core]
            x_send[j, d - 1] = (own + sib_recv[j, d].astype(jnp.float32)).astype(jnp.bfloat16)
            cross_copy(j, d).start()

    def out_copy(kind, j):
        held, out, width = ((att, att_out, per_head * HD), (gq, gq_out, per_head * HD),
                            (grk_low, grk_out, HD), (grv_low, grv_out, HD))[kind]
        return local(held.at[:, cols(j, width)], out.at[0, 0, :, cols(j, width)], out_sem.at[kind, j])

    def stacked(buf, j):
        return jnp.concatenate([buf[:, cols(j * per_head + h)] for h in range(per_head)], axis=0)

    def heads(back, fore, back_bufs, fore_bufs):
        if fore is not None:
            s = dot(kall[:, cols(fore)], stacked(qbuf, fore), NT)
        if back is not None:
            p_back = back_bufs[0][...]
            dv = dot(p_back, stacked(obuf, back), NN) * adv_row
            o_t = dot(vall[:, cols(back)], p_back, TN)
        if fore is not None:
            s = jnp.concatenate([s[:prompt], jnp.where(causal, s[prompt:], -1e30)], axis=0)
            top = jnp.max(s, axis=0, keepdims=True)
            e = jnp.exp2((s - top) * (score_scale * LOG2E))
            p = e * (1.0 / jnp.sum(e, axis=0, keepdims=True))
            fore_bufs[0][...] = p.astype(jnp.bfloat16)
            dp = dot(vall[:, cols(fore)], stacked(obuf, fore), NT)
        if back is not None:
            ds_back = back_bufs[1][...]
            dk = dot(ds_back, stacked(qbuf, back), NN) * (adv_row * score_scale)
            dq_t = dot(kall[:, cols(back)], ds_back, TN) * (adv_one * score_scale)
        if fore is not None:
            delta = jnp.sum(p * dp, axis=0, keepdims=True)
            fore_bufs[1][...] = (p * (dp - delta)).astype(jnp.bfloat16)
        if back is not None:
            part[back, :, :, :HD] = dk[:prompt].reshape(members, rows, HD)
            part[back, :, :, HD:] = dv[:prompt].reshape(members, rows, HD)
            for d in range(chips):
                sib_send[back, d] = part[back, chip_at(d) * 2 + (1 - core)].astype(jnp.bfloat16)
            sib_copy(back).start()
            grk[:, cols(back)] = dk[prompt:]
            grv[:, cols(back)] = dv[prompt:]
            o_t = jnp.where(live_lane, o_t, 0.0).astype(jnp.bfloat16)
            dq_t = dq_t.astype(jnp.bfloat16)
            for h in range(per_head):
                att[:, cols(back * per_head + h)] = o_t[:, h * slots:(h + 1) * slots].T
                gq[:, cols(back * per_head + h)] = dq_t[:, h * slots:(h + 1) * slots].T
            out_copy(0, back).start()

    bufs = ((probs0, dsc0), (probs1, dsc1))
    wait_head(0)
    for side in range(2):
        for d in range(1, chips):
            arrival(side, 0, chip_at(d) * 2 + core).wait_recv()
    forward_head(1)
    heads(None, 0, None, bufs[0])
    for step in range(1, members):
        owner = lax.rem(me + step, members)
        remote(stat_send, stat.at[owner], s_send.at[0], s_recv.at[owner], group, owner).wait_recv()
    tok_send[0] = functools.reduce(jnp.add, [stat[i, 0] for i in range(members)])
    tok_copy(0).start()
    reward_total = functools.reduce(jnp.add, [stat[i, 1] for i in range(members)])
    advantage = stat_send[1] - reward_total / members
    adv_row = advantage[0:1]
    adv_one = adv_row[:, 0:1]

    def pair(i, carry):
        j = 2 * i
        forward_head(j + 2)
        wait_head(j + 1)
        heads(j, j + 1, bufs[0], bufs[1])

        @pl.when(i > 0)
        def _():
            cross_head(j - 1)

        @pl.when(i == 0)
        def _():
            tok_copy(0).wait_recv()
            tok[3] = tok_send[0] + tok[0]

        relay(j)
        forward_head(j + 3)
        wait_head(j + 2)
        heads(j + 1, j + 2, bufs[1], bufs[0])
        cross_head(j)
        relay(j + 1)
        return carry

    lax.fori_loop(0, KVH // 2 - 1, pair, 0)
    wait_head(KVH - 1)
    heads(KVH - 2, KVH - 1, bufs[0], bufs[1])
    cross_head(KVH - 3)
    heads(KVH - 1, None, bufs[1], None)
    cross_head(KVH - 2)
    for slot in range(KVH - 2, nodes):
        relay(slot)
    tokens = tok[3]
    before = jnp.where(node > 0, tok_send[1] - tok[3], jnp.zeros_like(tokens))
    after = jnp.where(node < nodes - 1, tok_send[2] - tok[3], jnp.zeros_like(tokens))
    tokens = tokens + before + after
    factor = (float(slots * groups * members) / tokens)[0:1]
    factor_one = factor[:, 0:1]

    def scale_head(j, carry):
        span = cols(j, per_head * HD)
        gq[:, span] = (gq[:, span].astype(jnp.float32) * factor_one).astype(jnp.bfloat16)
        grk_low[:, cols(j)] = (grk[:, cols(j)] * factor).astype(jnp.bfloat16)
        grv_low[:, cols(j)] = (grv[:, cols(j)] * factor).astype(jnp.bfloat16)
        for kind in range(1, 4):
            out_copy(kind, j).start()
        return carry

    lax.fori_loop(0, KVH // 2, scale_head, 0)
    cross_head(KVH - 1)
    lax.fori_loop(KVH // 2, KVH, scale_head, 0)

    def finish(j, carry):
        total = part[j, me] + sib_recv[j, 0].astype(jnp.float32)
        for d in range(1, chips):
            cross_copy(j, d).wait_recv()
            total = total + x_recv[j, d - 1].astype(jnp.float32)
        gpk[:, cols(j)] = (total[:, :HD] * factor).astype(jnp.bfloat16)
        gpv[:, cols(j)] = (total[:, HD:] * factor).astype(jnp.bfloat16)
        return carry

    lax.fori_loop(0, KVH, finish, 0)
    ends = [local(gpk, gpk_out.at[0], end_sem.at[0]), local(gpv, gpv_out.at[0], end_sem.at[1])]
    for copy in ends:
        copy.start()

    def drain(j, carry):
        for side in range(2):
            for slot in range(chips):
                direct(side, j, slot).wait_send()
            for d in range(1, chips):
                forward(side, j, d).wait_send()
        sib_copy(j).wait_send()
        for d in range(1, chips):
            cross_copy(j, d).wait_send()
        for kind in range(4):
            out_copy(kind, j).wait()
        return carry

    lax.fori_loop(0, KVH, drain, 0)
    for step in range(1, members):
        stat_copy(step).wait_send()
    tok_copy(0).wait_send()

    @pl.when(node < nodes - 1)
    def _():
        tok_copy(1).wait_send()

    @pl.when(node > 0)
    def _():
        tok_copy(2).wait_send()

    for copy in ends:
        copy.wait()


def place_kernel(*refs):
    count = len(refs) // 3
    sem = refs[-1]
    ins, outs = [], []
    for i in range(count):
        source, out, held = refs[i], refs[count + i], refs[2 * count + i]
        tall = source.shape[-2]
        pieces = 2 if source.shape[-1] > KVH * HD else 1
        for piece in range(pieces):
            span = pl.ds(piece * (tall // pieces), tall // pieces)
            index = (0,) * (len(source.shape) - 2) + (span,)
            spot = len(ins)
            ins.append(pltpu.make_async_copy(source.at[index], held.at[span], sem.at[0, spot]))
            outs.append(pltpu.make_async_copy(held.at[span], out.at[index], sem.at[1, spot]))
    for copy in ins:
        copy.start()
    for copy_in, copy_out in zip(ins, outs):
        copy_in.wait()
        copy_out.start()
    for copy in outs:
        copy.wait()


def body(prompt_k, prompt_v, resp_q, resp_k, resp_v, out_grad, lengths, rewards):
    members = lax.axis_size("member")
    groups = lax.axis_size("group")
    chips = members // 2
    rows = prompt_k.shape[1]
    slots = resp_q.shape[2]
    per_head = resp_q.shape[3] // (KVH * HD)
    keys = members * rows + slots
    width = KVH * HD
    bf, f32 = jnp.bfloat16, jnp.float32
    dma = pltpu.SemaphoreType.DMA
    crossing = max(chips - 1, 1)
    scratch = [
        pltpu.VMEM((keys, width), bf),
        pltpu.VMEM((keys, width), bf),
        pltpu.VMEM((slots, width * per_head), bf),
        pltpu.VMEM((slots, width * per_head), bf),
        pltpu.VMEM((slots, width * per_head), bf),
        pltpu.VMEM((slots, width * per_head), bf),
        pltpu.VMEM((slots, width), f32),
        pltpu.VMEM((slots, width), f32),
        pltpu.VMEM((slots, width), bf),
        pltpu.VMEM((slots, width), bf),
        pltpu.VMEM((rows, width), bf),
        pltpu.VMEM((rows, width), bf),
        pltpu.VMEM((keys, slots * per_head), bf),
        pltpu.VMEM((keys, slots * per_head), bf),
        pltpu.VMEM((keys, slots * per_head), bf),
        pltpu.VMEM((keys, slots * per_head), bf),
        pltpu.VMEM((KVH, members, rows, 2 * HD), f32),
        pltpu.VMEM((KVH, chips, rows, 2 * HD), bf),
        pltpu.VMEM((KVH, chips, rows, 2 * HD), bf),
        pltpu.VMEM((KVH, crossing, rows, 2 * HD), bf),
        pltpu.VMEM((KVH, crossing, rows, 2 * HD), bf),
        pltpu.VMEM((2, 8, HD), f32),
        pltpu.VMEM((members, 2, 8, HD), f32),
        pltpu.VMEM((3, 8, HD), f32),
        pltpu.VMEM((4, 8, HD), f32),
        dma((6,)),
        dma((2, KVH, chips)),
        dma((2, KVH, crossing)),
        dma((2, KVH, members)),
        dma((members,)),
        dma((members,)),
        dma((3,)),
        dma((3,)),
        dma((KVH,)),
        dma((KVH,)),
        dma((KVH, crossing)),
        dma((KVH, crossing)),
        dma((4, KVH)),
        dma((2,)),
    ]
    held = pl.BlockSpec(memory_space=pl.ANY)
    scalar = pl.BlockSpec(memory_space=pltpu.SMEM)
    stored = pl.BlockSpec(memory_space=pltpu.HBM)
    flops = 10 * slots * width * per_head * keys
    moved = sum(2 * a.size * a.dtype.itemsize for a in (resp_q, out_grad, resp_k, resp_v, prompt_k, prompt_v))
    results = pl.pallas_call(
        functools.partial(kernel, groups, members, rows, slots, per_head),
        out_shape=[
            jax.ShapeDtypeStruct(a.shape, bf) for a in (resp_q, resp_q, resp_k, resp_v, prompt_k, prompt_v)
        ],
        in_specs=[scalar, scalar] + [stored] * 6,
        out_specs=[held] * 6,
        scratch_shapes=scratch,
        compiler_params=pltpu.CompilerParams(
            collective_id=0, has_side_effects=True, vmem_limit_bytes=60 * 1024 * 1024),
        cost_estimate=pl.CostEstimate(
            flops=flops, bytes_accessed=moved, transcendentals=slots * KVH * per_head * keys),
        name="shared_prompt_attention",
    )(lengths, rewards, prompt_k, prompt_v, resp_q, resp_k, resp_v, out_grad)
    return pl.pallas_call(
        place_kernel,
        out_shape=[jax.ShapeDtypeStruct(a.shape, bf) for a in results],
        in_specs=[stored] * 6,
        out_specs=[stored] * 6,
        scratch_shapes=[pltpu.VMEM(a.shape[-2:], bf) for a in results] + [dma((2, 8))],
        compiler_params=pltpu.CompilerParams(vmem_limit_bytes=60 * 1024 * 1024),
        cost_estimate=pl.CostEstimate(flops=0, bytes_accessed=moved, transcendentals=0),
        name="place_results",
    )(*results)


def solution(mesh):
    rows = P("group", "member", None)
    wide = P("group", "member", None, None)
    return jax.shard_map(
        body,
        mesh=mesh,
        in_specs=(rows, rows, wide, wide, wide, wide, P("group", "member"), P("group", "member")),
        out_specs=(wide, wide, wide, wide, rows, rows),
        check_vma=False,
    )
```

profile of v0, /device:TPU:0, one launch (start us, length us, event | category | flops | bytes accessed | tf_op | source)
XLA Modules:
  0.0 36.2 jit_solution(4315028510541847833)
XLA Ops:
  1.9 31.5 %shared_prompt_attention.1 = (bf16[1,1,128,4096]{3,2,1,0:T(8,128)(2,1)}, bf16[1,1,128,4096]{3,2,1,0:T(8,128)(2,1)}, bf16[1,1,128,1024]{3,2,1,0:T(8,128)(2,1)}, b...) custom-call(s32[1,1]{1,0:T(1,128)S(6)} %copy.14.length_ref, ...), custom_call_target="tpu_custom_call" | custom-call | flops 2013265920 | bytes 5767168 | tf_op jit(solution)/shard_map/shared_prompt_attention/pallas_call | solution.py:449
  33.4 2.7 %place_results.1 = (bf16[1,1,128,4096]{3,2,1,0:T(8,128)(2,1)}, bf16[1,1,128,4096]{3,2,1,0:T(8,128)(2,1)}, bf16[1,1,128,1024]{3,2,1,0:T(8,128)(2,1)}, bf16[1,1,12...) custom-call(bf16[1,1,128,4096]{3,2,1,0:T(8,128)(2,1)} %get-tuple-element.12.refs_0_, ...), custom_call_target="tpu_custom_call" | custom-call | bytes 5767168 | tf_op jit(solution)/shard_map/place_results/pallas_call | solution.py:463
where the time goes:
time: 36.4 us; the launch traced here: 36.2 us
  Pallas kernels  34.2 us (94%)
  between operations  1.93 us (5%)
    pallas_call x1, Pallas kernels, body(): pl.pallas_call(functools.partial(kernel, groups, members, rows, slots, pe...  31.5 us
    pallas_call x1, Pallas kernels, body(): pl.pallas_call(place_kernel, out_shape=[jax.ShapeDtypeStruct(a.shape, bf)...  2.74 us

commit v1 on v0

--- a/solution.py
+++ b/solution.py
@@ -117,7 +117,7 @@
         return remote(tok_send.at[kind], tok.at[kind], t_send.at[kind], t_recv.at[kind], to, me)
 
     def relay(slot):
-        @pl.when(node == slot)
+        @pl.when(2 * node == slot)
         def _():
             @pl.when(node > 0)
             def _():
@@ -132,7 +132,7 @@
             def _():
                 tok_copy(1).start()
 
-        @pl.when(node == nodes - 1 - slot)
+        @pl.when(2 * (nodes - 1 - node) == slot)
         def _():
             @pl.when(node < nodes - 1)
             def _():
@@ -201,6 +201,11 @@
     def cross_copy(j, d):
         return remote(x_send.at[j, d - 1], x_recv.at[j, d - 1], c_send.at[j, d - 1], c_recv.at[j, d - 1],
                       group, chip_at(d) * 2 + core)
+
+    def send_part(j):
+        for d in range(chips):
+            sib_send[j, d] = part[j, chip_at(d) * 2 + (1 - core)].astype(jnp.bfloat16)
+        sib_copy(j).start()
 
     def cross_head(j):
         sib_copy(j).wait_recv()
@@ -241,9 +246,8 @@
         if back is not None:
             part[back, :, :, :HD] = dk[:prompt].reshape(members, rows, HD)
             part[back, :, :, HD:] = dv[:prompt].reshape(members, rows, HD)
-            for d in range(chips):
-                sib_send[back, d] = part[back, chip_at(d) * 2 + (1 - core)].astype(jnp.bfloat16)
-            sib_copy(back).start()
+            if fore is None:
+                send_part(back)
             grk[:, cols(back)] = dk[prompt:]
             grv[:, cols(back)] = dv[prompt:]
             o_t = jnp.where(live_lane, o_t, 0.0).astype(jnp.bfloat16)
@@ -251,6 +255,8 @@
             for h in range(per_head):
                 att[:, cols(back * per_head + h)] = o_t[:, h * slots:(h + 1) * slots].T
                 gq[:, cols(back * per_head + h)] = dq_t[:, h * slots:(h + 1) * slots].T
+            if fore is not None:
+                send_part(back)
             out_copy(0, back).start()
 
     bufs = ((probs0, dsc0), (probs1, dsc1))
@@ -299,7 +305,7 @@
     cross_head(KVH - 3)
     heads(KVH - 1, None, bufs[1], None)
     cross_head(KVH - 2)
-    for slot in range(KVH - 2, nodes):
+    for slot in range(KVH - 2, 2 * nodes - 1):
         relay(slot)
     tokens = tok[3]
     before = jnp.where(node > 0, tok_send[1] - tok[3], jnp.zeros_like(tokens))

time: 36.4 us -> 31.9 us (0.88)
  Pallas kernels: 34.2 us -> 29.8 us
    pallas_call x1, Pallas kernels: 31.5 us -> 27.1 us  [body(): pl.pallas_call(functools.partial(kernel, groups, members, rows, slots, pe...]
where the time goes in v1:
time: 31.9 us; the launch traced here: 31.7 us
  Pallas kernels  29.8 us (93%)
  between operations  1.93 us (6%)
    pallas_call x1, Pallas kernels, body(): pl.pallas_call(functools.partial(kernel, groups, members, rows, slots, pe...  27.1 us
    pallas_call x1, Pallas kernels, body(): pl.pallas_call(place_kernel, out_shape=[jax.ShapeDtypeStruct(a.shape, bf)...  2.74 us

profile of v1, /device:TPU:0, one launch (start us, length us, event | category | flops | bytes accessed | tf_op | source)
XLA Modules:
  0.0 31.7 jit_solution(13281959966167020292)
XLA Ops:
  1.9 27.1 %shared_prompt_attention.1 = (bf16[1,1,128,4096]{3,2,1,0:T(8,128)(2,1)}, bf16[1,1,128,4096]{3,2,1,0:T(8,128)(2,1)}, bf16[1,1,128,1024]{3,2,1,0:T(8,128)(2,1)}, b...) custom-call(s32[1,1]{1,0:T(1,128)S(6)} %copy.14.length_ref, ...), custom_call_target="tpu_custom_call" | custom-call | flops 2013265920 | bytes 5767168 | tf_op jit(solution)/shard_map/shared_prompt_attention/pallas_call | solution.py:455
  29.0 2.7 %place_results.1 = (bf16[1,1,128,4096]{3,2,1,0:T(8,128)(2,1)}, bf16[1,1,128,4096]{3,2,1,0:T(8,128)(2,1)}, bf16[1,1,128,1024]{3,2,1,0:T(8,128)(2,1)}, bf16[1,1,12...) custom-call(bf16[1,1,128,4096]{3,2,1,0:T(8,128)(2,1)} %get-tuple-element.12.refs_0_, ...), custom_call_target="tpu_custom_call" | custom-call | bytes 5767168 | tf_op jit(solution)/shard_map/place_results/pallas_call | solution.py:469

commit v2 on v1

--- a/solution.py
+++ b/solution.py
@@ -76,21 +76,14 @@
     twin = node * 2 + (1 - lax.rem(group, 2))
     pl.semaphore_signal(barrier, inc=1, device_id=(twin, me), device_id_type=MESH)
 
-    @pl.when(node > 0)
-    def _():
-        pl.semaphore_signal(barrier, inc=1, device_id=(group - 2, me), device_id_type=MESH)
-
-    @pl.when(node < nodes - 1)
-    def _():
-        pl.semaphore_signal(barrier, inc=1, device_id=(group + 2, me), device_id_type=MESH)
-
+    for step in range(1, nodes):
+        pl.semaphore_signal(barrier, inc=1, device_id=(lax.rem(group + 2 * step, groups), me), device_id_type=MESH)
 
     length = length_ref[0, 0]
     stat_send[0] = jnp.full((8, HD), length.astype(jnp.float32))
     stat_send[1] = jnp.full((8, HD), reward_ref[0, 0])
     stat[me] = stat_send[...]
-    ends = (node == 0).astype(jnp.int32) + (node == nodes - 1).astype(jnp.int32)
-    pl.semaphore_wait(barrier, members + 2 - ends)
+    pl.semaphore_wait(barrier, members + nodes - 1)
 
     sides = ((pk_ref, kall), (pv_ref, vall))
 
@@ -112,40 +105,12 @@
     def stat_copy(step):
         return remote(stat_send, stat.at[me], s_send.at[step - 1], s_recv.at[me], group, lax.rem(me + step, members))
 
-    def tok_copy(kind):
-        to = (twin, group + 2, group - 2)[kind]
-        return remote(tok_send.at[kind], tok.at[kind], t_send.at[kind], t_recv.at[kind], to, me)
-
-    def relay(slot):
-        @pl.when(2 * node == slot)
-        def _():
-            @pl.when(node > 0)
-            def _():
-                tok_copy(1).wait_recv()
-                tok_send[1] = tok[1] + tok[3]
-
-            @pl.when(node == 0)
-            def _():
-                tok_send[1] = tok[3]
-
-            @pl.when(node < nodes - 1)
-            def _():
-                tok_copy(1).start()
-
-        @pl.when(2 * (nodes - 1 - node) == slot)
-        def _():
-            @pl.when(node < nodes - 1)
-            def _():
-                tok_copy(2).wait_recv()
-                tok_send[2] = tok[2] + tok[3]
-
-            @pl.when(node == nodes - 1)
-            def _():
-                tok_send[2] = tok[3]
-
-            @pl.when(node > 0)
-            def _():
-                tok_copy(2).start()
+    def twin_copy():
+        return remote(tok_send.at[0], tok.at[nodes], t_send.at[0], t_recv.at[nodes], twin, me)
+
+    def tok_copy(step):
+        return remote(tok_send.at[1], tok.at[node], t_send.at[step], t_recv.at[node],
+                      lax.rem(group + 2 * step, groups), me)
 
     def far(side, d):
         source, whole = sides[side]
@@ -270,7 +235,7 @@
         owner = lax.rem(me + step, members)
         remote(stat_send, stat.at[owner], s_send.at[0], s_recv.at[owner], group, owner).wait_recv()
     tok_send[0] = functools.reduce(jnp.add, [stat[i, 0] for i in range(members)])
-    tok_copy(0).start()
+    twin_copy().start()
     reward_total = functools.reduce(jnp.add, [stat[i, 1] for i in range(members)])
     advantage = stat_send[1] - reward_total / members
     adv_row = advantage[0:1]
@@ -288,15 +253,16 @@
 
         @pl.when(i == 0)
         def _():
-            tok_copy(0).wait_recv()
-            tok[3] = tok_send[0] + tok[0]
-
-        relay(j)
+            twin_copy().wait_recv()
+            tok_send[1] = tok_send[0] + tok[nodes]
+            tok[node] = tok_send[1]
+            for step in range(1, nodes):
+                tok_copy(step).start()
+
         forward_head(j + 3)
         wait_head(j + 2)
         heads(j + 1, j + 2, bufs[1], bufs[0])
         cross_head(j)
-        relay(j + 1)
         return carry
 
     lax.fori_loop(0, KVH // 2 - 1, pair, 0)
@@ -305,12 +271,10 @@
     cross_head(KVH - 3)
     heads(KVH - 1, None, bufs[1], None)
     cross_head(KVH - 2)
-    for slot in range(KVH - 2, 2 * nodes - 1):
-        relay(slot)
-    tokens = tok[3]
-    before = jnp.where(node > 0, tok_send[1] - tok[3], jnp.zeros_like(tokens))
-    after = jnp.where(node < nodes - 1, tok_send[2] - tok[3], jnp.zeros_like(tokens))
-    tokens = tokens + before + after
+    for step in range(1, nodes):
+        owner = lax.rem(node + step, nodes)
+        remote(tok_send.at[1], tok.at[owner], t_send.at[0], t_recv.at[owner], twin, me).wait_recv()
+    tokens = functools.reduce(jnp.add, [tok[i] for i in range(nodes)])
     factor = (float(slots * groups * members) / tokens)[0:1]
     factor_one = factor[:, 0:1]
 
@@ -357,16 +321,9 @@
     lax.fori_loop(0, KVH, drain, 0)
     for step in range(1, members):
         stat_copy(step).wait_send()
-    tok_copy(0).wait_send()
-
-    @pl.when(node < nodes - 1)
-    def _():
-        tok_copy(1).wait_send()
-
-    @pl.when(node > 0)
-    def _():
-        tok_copy(2).wait_send()
-
+    twin_copy().wait_send()
+    for step in range(1, nodes):
+        tok_copy(step).wait_send()
     for copy in ends:
         copy.wait()
 
@@ -430,16 +387,16 @@
         pltpu.VMEM((KVH, crossing, rows, 2 * HD), bf),
         pltpu.VMEM((2, 8, HD), f32),
         pltpu.VMEM((members, 2, 8, HD), f32),
-        pltpu.VMEM((3, 8, HD), f32),
-        pltpu.VMEM((4, 8, HD), f32),
+        pltpu.VMEM((2, 8, HD), f32),
+        pltpu.VMEM((groups // 2 + 1, 8, HD), f32),
         dma((6,)),
         dma((2, KVH, chips)),
         dma((2, KVH, crossing)),
         dma((2, KVH, members)),
         dma((members,)),
         dma((members,)),
-        dma((3,)),
-        dma((3,)),
+        dma((groups // 2,)),
+        dma((groups // 2 + 1,)),
         dma((KVH,)),
         dma((KVH,)),
         dma((KVH, crossing)),

time: 31.9 us -> 32.4 us (1.016)
  Pallas kernels: 29.8 us -> 30.3 us
    pallas_call x1, Pallas kernels: 27.1 us -> 27.5 us  [body(): pl.pallas_call(functools.partial(kernel, groups, members, rows, slots, pe...]
where the time goes in v2:
time: 32.4 us; the launch traced here: 32.2 us
  Pallas kernels  30.3 us (94%)
  between operations  1.93 us (6%)
    pallas_call x1, Pallas kernels, body(): pl.pallas_call(functools.partial(kernel, groups, members, rows, slots, pe...  27.5 us
    pallas_call x1, Pallas kernels, body(): pl.pallas_call(place_kernel, out_shape=[jax.ShapeDtypeStruct(a.shape, bf)...  2.74 us

profile of v2, /device:TPU:0, one launch (start us, length us, event | category | flops | bytes accessed | tf_op | source)
XLA Modules:
  0.0 32.2 jit_solution(9623196483792314864)
XLA Ops:
  1.9 27.5 %shared_prompt_attention.1 = (bf16[1,1,128,4096]{3,2,1,0:T(8,128)(2,1)}, bf16[1,1,128,4096]{3,2,1,0:T(8,128)(2,1)}, bf16[1,1,128,1024]{3,2,1,0:T(8,128)(2,1)}, b...) custom-call(s32[1,1]{1,0:T(1,128)S(6)} %copy.14.length_ref, ...), custom_call_target="tpu_custom_call" | custom-call | flops 2013265920 | bytes 5767168 | tf_op jit(solution)/shard_map/shared_prompt_attention/pallas_call | solution.py:412
  29.4 2.7 %place_results.1 = (bf16[1,1,128,4096]{3,2,1,0:T(8,128)(2,1)}, bf16[1,1,128,4096]{3,2,1,0:T(8,128)(2,1)}, bf16[1,1,128,1024]{3,2,1,0:T(8,128)(2,1)}, bf16[1,1,12...) custom-call(bf16[1,1,128,4096]{3,2,1,0:T(8,128)(2,1)} %get-tuple-element.12.refs_0_, ...), custom_call_target="tpu_custom_call" | custom-call | bytes 5767168 | tf_op jit(solution)/shard_map/place_results/pallas_call | solution.py:426

commit v3 on v1

--- a/solution.py
+++ b/solution.py
@@ -305,6 +305,7 @@
     cross_head(KVH - 3)
     heads(KVH - 1, None, bufs[1], None)
     cross_head(KVH - 2)
+    cross_head(KVH - 1)
     for slot in range(KVH - 2, 2 * nodes - 1):
         relay(slot)
     tokens = tok[3]
@@ -323,9 +324,7 @@
             out_copy(kind, j).start()
         return carry
 
-    lax.fori_loop(0, KVH // 2, scale_head, 0)
-    cross_head(KVH - 1)
-    lax.fori_loop(KVH // 2, KVH, scale_head, 0)
+    lax.fori_loop(0, KVH, scale_head, 0)
 
     def finish(j, carry):
         total = part[j, me] + sib_recv[j, 0].astype(jnp.float32)

time: 31.9 us -> 30.7 us (0.962)
  the two profiles are of different devices: /device:TPU:0 before, /device:TPU:9 now
where the time goes in v3:
time: 30.7 us; the launch traced here: 30.6 us
  Pallas kernels  28.6 us (93%)
  between operations  1.93 us (6%)
    pallas_call x1, Pallas kernels, body(): pl.pallas_call(functools.partial(kernel, groups, members, rows, slots, pe...  25.9 us
    pallas_call x1, Pallas kernels, body(): pl.pallas_call(place_kernel, out_shape=[jax.ShapeDtypeStruct(a.shape, bf)...  2.74 us

profile of v3, /device:TPU:9, one launch (start us, length us, event | category | flops | bytes accessed | tf_op | source)
XLA Modules:
  0.0 30.6 jit_solution(17121940097681243787)
XLA Ops:
  1.9 25.9 %shared_prompt_attention.1 = (bf16[1,1,128,4096]{3,2,1,0:T(8,128)(2,1)}, bf16[1,1,128,4096]{3,2,1,0:T(8,128)(2,1)}, bf16[1,1,128,1024]{3,2,1,0:T(8,128)(2,1)}, b...) custom-call(s32[1,1]{1,0:T(1,128)S(6)} %copy.14.length_ref, ...), custom_call_target="tpu_custom_call" | custom-call | flops 2013265920 | bytes 5767168 | tf_op jit(solution)/shard_map/shared_prompt_attention/pallas_call | solution.py:454
  27.8 2.7 %place_results.1 = (bf16[1,1,128,4096]{3,2,1,0:T(8,128)(2,1)}, bf16[1,1,128,4096]{3,2,1,0:T(8,128)(2,1)}, bf16[1,1,128,1024]{3,2,1,0:T(8,128)(2,1)}, bf16[1,1,12...) custom-call(bf16[1,1,128,4096]{3,2,1,0:T(8,128)(2,1)} %get-tuple-element.12.refs_0_, ...), custom_call_target="tpu_custom_call" | custom-call | bytes 5767168 | tf_op jit(solution)/shard_map/place_results/pallas_call | solution.py:468
